TPU v7x, 32 devices: a whole 2x2x4 slice. The times are simulated.
32 devices in a mesh: dp: 8 (over z, x), tensor: 4 (over y, core).
Axes of the slice: x: 2, y: 2, z: 4, core: 2. Of those that a mesh axis runs over, the one named last changes fastest.
Arguments:
- grads: bfloat16 [8, 1024, 12288], P('dp', 'tensor'), may hold values from -65 to 65
- errors: bfloat16 [8, 1024, 12288], P('dp', 'tensor'), may hold values from -4 to 4
- q_init: float32 [4, 12288], replicated, may hold values from -6 to 6
- bias_grads: float32 [8, 12288], P('dp', 'tensor'), may hold values from -6 to 6
- head_group: int32 [96, 1], replicated, may hold values from 0 to 7
Outputs:
- new_errors: bfloat16 [8, 1024, 12288], P('dp', 'tensor')
- p_factor: float32 [4, 1024], P(None, 'tensor')
- q_factor: float32 [4, 12288], replicated
- bias_update: float32 [1024], P('tensor')
Inputs may be any that keep to these rules, and one draw needn't show every extreme that they name: `head_group`: every group is named by at least one query head.
All inputs are finite; a program needn't handle non-finite values.
Results may differ from a plain program's by a relative error of at most 0.001.
Values sent between devices are 32-bit elements; how exact they have to be, the bound alone decides.
No kernel may reach another device: no remote copies, remote signals or barrier semaphores. Data moves between devices by JAX's collectives and lax.ppermute only.
A program may use at most 64 MiB of HBM per device.

v0:
```python
import jax
import jax.numpy as jnp
from jax import lax
from jax.sharding import PartitionSpec as P

HD = 128
NG = 8


def per_device(grads, errors, q_init, bias_grads, head_group):
    highest = lax.Precision.HIGHEST
    replicas = lax.axis_size("dp")
    shard_idx = lax.axis_index("tensor")
    merged = grads[0].astype(jnp.float32) + errors[0].astype(jnp.float32)
    local_rows = merged.shape[0]
    p_part = lax.dot_general(q_init, merged, (((1,), (1,)), ((), ())), precision=highest)
    local_heads = bias_grads.shape[1] // HD
    groups = head_group[:, 0]
    group_ids = jnp.arange(NG, dtype=jnp.int32)
    onehot_all = (groups[None, :] == group_ids[:, None]).astype(jnp.float32)
    counts = jnp.sum(onehot_all, axis=1)
    local_groups = lax.dynamic_slice_in_dim(groups, shard_idx * local_heads, local_heads)
    onehot_local = (local_groups[None, :] == group_ids[:, None]).astype(jnp.float32)
    bias_part = jnp.dot(onehot_local, bias_grads[0].reshape(local_heads, HD), precision=highest)
    p_own = lax.psum(p_part, "dp") / replicas
    gram_local = jnp.dot(p_own, p_own.T, precision=highest)
    gram_matrix = lax.psum(gram_local, "tensor")
    chol_lower = jnp.linalg.cholesky(gram_matrix)
    p_factor = jax.scipy.linalg.solve_triangular(chol_lower, p_own, lower=True)
    q_part = jnp.dot(p_factor, merged, precision=highest)
    q_total, bias_total = lax.psum((q_part, bias_part), ("dp", "tensor"))
    q_factor = q_total / replicas
    approx = lax.dot_general(p_factor, q_factor, (((0,), (0,)), ((), ())), precision=highest)
    new_errors = (merged - approx).astype(jnp.bfloat16)[None]
    pooled = bias_total / (counts[:, None] * replicas)
    flat_bias = pooled.reshape(-1)
    bias_update = lax.dynamic_slice_in_dim(flat_bias, shard_idx * local_rows, local_rows)
    return (new_errors, p_factor, q_factor, bias_update)


def solution(mesh):
    placed = (P("dp", "tensor", None), P("dp", "tensor", None), P(), P("dp", "tensor"), P())
    return jax.shard_map(
        per_device,
        mesh=mesh,
        in_specs=placed,
        out_specs=(P("dp", "tensor", None), P(None, "tensor"), P(), P("tensor")),
        check_vma=False,
    )
```

profile of v0, /device:TPU:1, one launch (start us, length us, event | category | flops | bytes accessed | tf_op | source)
XLA Modules:
  0.0 205.9 jit_solution(10697461204546558248)
XLA Ops:
  7.2 0.0 copy-start
  7.2 0.0 all-reduce.2.cloned.1.call-start
  7.2 0.9 copy-done
  8.1 13.2 %fusion.6 = f32[4,256]{1,0:T(4,128)S(1)} fusion(f32[4,12288]{1,0:T(4,128)S(1)} %copy-done, bf16[1,256,12288]{2,1,0:T(8,128)(2,1)} %param.6, bf16[1,256,12288]{2,1,0:T(8,128)(2,1)} %param.5), kind=kOutput, calls=%fused_computation.8 | convolution fusion | flops 160432128 | bytes 12783616 | tf_op jit(solution)/shard_map/dot_general | solution.py:16
  21.3 18.7 %psum.28 = f32[4,256]{1,0:T(4,128)S(1)} all-reduce(f32[4,256]{1,0:T(4,128)S(1)} %fusion.6), channel_id=1, replica_groups=mesh['dp'=8,'tensor'=4] {'dp'}, use_global_device_ids=true, to_apply=%region_0.0 | all-reduce | flops 1024 | bytes 8192 | tf_op jit(solution)/shard_map/psum | solution.py:25
  40.1 0.1 fusion.12
  40.2 9.4 %psum.29 = f32[4,4]{0,1:T(4,128)S(1)} all-reduce(f32[4,4]{0,1:T(4,128)S(1)} %fusion.12), channel_id=1, replica_groups=mesh['dp'=8,'tensor'=4] {'tensor'}, use_global_device_ids=true, to_apply=%region_1.0 | all-reduce | flops 16 | bytes 128 | tf_op jit(solution)/shard_map/psum | solution.py:27
  49.6 0.1 copy.13
  49.7 0.4 cholesky.16
  50.1 0.6 compare_reduce_fusion
  50.8 0.6 fusion.14
  51.4 0.3 custom-call.7
  51.8 0.2 fusion.10
  52.0 10.6 %fusion.2 = f32[4,12288]{1,0:T(4,128)} fusion(f32[4,256]{1,0:T(4,128)S(1)} %fusion.10, bf16[1,256,12288]{2,1,0:T(8,128)(2,1)} %param.6, bf16[1,256,12288]{2,1,0:T(8,128)(2,1)} %param.5), kind=kOutput, calls=%fused_computation.3 | convolution fusion | flops 160432128 | bytes 12783616 | tf_op jit(solution)/shard_map/dot_general | solution.py:30
  62.6 0.0 all-reduce.2.cloned.1.call-update
  62.6 0.1 dynamic-slice_bitcast_fusion
  62.7 0.1 convert_reduce_fusion
  62.8 0.1 fusion.9
  63.0 36.2 %psum.31 = f32[8,128]{1,0:T(8,128)S(1)} all-reduce(f32[8,128]{1,0:T(8,128)S(1)} %fusion.9), channel_id=1, replica_groups=mesh['dp'=8,'tensor'=4] {'dp','tensor'}, use_global_device_ids=true, to_apply=%region_5.6 | all-reduce | flops 1024 | bytes 8192 | tf_op jit(solution)/shard_map/psum | solution.py:31
  99.2 0.1 divide_bitcast_fusion
  99.2 0.6 dynamic_slice.7
  99.9 82.9 %all-reduce.2.cloned.1.call-done = f32[4,12288]{1,0:T(4,128)} async-done(((f32[4,12288]{1,0:T(4,128)}), f32[4,12288]{1,0:T(4,128)}) %all-reduce.2.cloned.1.call-update) | async-done | bytes 196624 | tf_op jit(solution)/shard_map/psum | solution.py:31
  182.8 1.0 broadcast_multiply_fusion
  183.8 15.2 %fusion.1 = bf16[1,256,12288]{2,1,0:T(8,128)(2,1)} fusion(f32[4,256]{1,0:T(4,128)S(1)} %fusion.10, f32[4,12288]{1,0:T(4,128)S(1)} %broadcast_multiply_fusion, bf16[1,256,12288]{2,1,0:T(8,128)(2,1)} %param.6, bf16[1,256,12288]{2,1,0:T(8,128)(2,1)} %param.5), kind=kOutput, calls=%fused_computation.2 | convolution fusion | flops 166723584 | bytes 19075072 | tf_op jit(solution)/shard_map/dot_general | solution.py:33
  (11 shorter events, 0.1 us)
Async XLA Ops:
  7.2 0.9 copy-start
  7.2 175.6 %all-reduce.2.cloned.1.call-start = ((), (), s32[]{:S(2)}) async-start(), calls=%async_computation | async-start | bytes 393216 | tf_op jit(solution)/shard_map/psum | solution.py:31
  51.9 131.8 %copy-start.2 = (f32[4,256]{1,0:T(4,128)}, f32[4,256]{1,0:T(4,128)S(1)}, u32[]{:S(2)}) copy-start(f32[4,256]{1,0:T(4,128)S(1)} %fusion.10) | copy-start | bytes 12292
  52.0 10.7 %copy-start.4 = (s32[96,1]{0,1:T(1,128)S(1)}, s32[96,1]{0,1:T(1,128)}, u32[]{:S(2)}) copy-start(s32[96,1]{0,1:T(1,128)} %param.9) | copy-start | bytes 1156
  52.0 10.9 %copy-start.3 = (f32[1,3072]{1,0:T(1,128)S(1)}, f32[1,3072]{1,0:T(1,128)}, u32[]{:S(2)}) copy-start(f32[1,3072]{1,0:T(1,128)} %param.8) | copy-start | bytes 36868
  183.8 15.2 %copy-start.1 = (f32[4,12288]{1,0:T(4,128)}, f32[4,12288]{1,0:T(4,128)S(1)}, u32[]{:S(2)}) copy-start(f32[4,12288]{1,0:T(4,128)S(1)} %broadcast_multiply_fusion) | copy-start | bytes 589828
Sparse Core Ops, SparseCore 0:
  62.7 120.0 all-reduce.1
where the time goes:
time: 208 us; the launch traced here: 206 us
  waiting for transfers between devices  82.9 us (40%)
  blocking collectives  64.4 us (31%)
  matrix products  39.5 us (19%)
  between operations  14.1 us (7%)
  other arithmetic  3.19 us (2%)
    psum x1, waiting for transfers between devices, per_device(): q_total, bias_total = lax.psum((q_part, bias_part), ('dp', 'tensor'))  82.9 us
    psum x1, blocking collectives, per_device(): q_total, bias_total = lax.psum((q_part, bias_part), ('dp', 'tensor'))  36.2 us
    psum x1, blocking collectives, per_device(): p_own = lax.psum(p_part, 'dp') / replicas  18.7 us
    dot_general x1, matrix products, per_device(): lax.dot_general(p_factor, q_factor, (((0,), (0,)), ((), ())), precision=h...  15.2 us
    dot_general x1, matrix products, per_device(): lax.dot_general(q_init, merged, (((1,), (1,)), ((), ())), precision=highest)  13.2 us
    dot_general x1, matrix products, per_device(): q_part = jnp.dot(p_factor, merged, precision=highest)  10.6 us
    psum x1, blocking collectives, per_device(): gram_matrix = lax.psum(gram_local, 'tensor')  9.43 us
  transfers between devices with their start and end apart: 1, of which 1 were waited for; matrix products, arithmetic and copies ran while one was open for 0% of the time, Pallas kernels for 0%

commit v1 on v0

v1 whole, which is shorter than its diff:
```python
import functools
import math

import jax
import jax.numpy as jnp
from jax import lax
from jax.experimental import pallas as pl
from jax.experimental.pallas import tpu as pltpu
from jax.sharding import PartitionSpec as P

HD = 128
NG = 8
RANK = 4
LANES = 128
MIB = 1 << 20
F32 = jnp.float32
BF16 = jnp.bfloat16


def split3(x):
    high = x.astype(BF16).astype(F32)
    rest = x - high
    mid = rest.astype(BF16).astype(F32)
    return high, mid, rest - mid


def stack16(x):
    high, mid, low = split3(x)
    return jnp.concatenate([high, mid, low, jnp.zeros_like(x)], axis=0).astype(BF16)


def fold16(x):
    return (x[8:12] + x[4:8]) + x[0:4]


def butterfly_sum(parts):
    while len(parts) > 1:
        parts = [parts[i] + parts[i + 1] for i in range(0, len(parts), 2)]
    return parts[0]


def left_kernel(block, replicas, groups_hbm, q_hbm, bias_hbm, grads_hbm, errors_hbm, left_ref, bias_out, grads_ref, errors_ref, groups_ref, q_ref, q16_ref, wide_q, bias_ref, sums_ref, small_sems, sems):
    rows, width = grads_hbm.shape
    strip = 32
    blocks = rows // block
    split = width * 9 // 16
    fetch_q = pltpu.make_async_copy(q_hbm, q_ref, small_sems.at[0])
    fetch_groups = pltpu.make_async_copy(groups_hbm, groups_ref, small_sems.at[1])
    fetch_bias = pltpu.make_async_copy(bias_hbm, bias_ref, small_sems.at[2])
    fetch_q.start(priority=1)

    def fetches(b):
        at = pl.ds(b * block, block)
        return (
            pltpu.make_async_copy(grads_hbm.at[at], grads_ref.at[at], sems.at[0, b]),
            pltpu.make_async_copy(errors_hbm.at[at], errors_ref.at[at], sems.at[1, b]),
        )

    for b in range(blocks):
        for queue, copy in enumerate(fetches(b)):
            copy.start(priority=queue)
    fetch_groups.start(priority=0)
    fetch_bias.start(priority=1)
    fetch_q.wait()
    step = split // 3
    for k in range(0, split, step):
        q16_ref[:, k : k + step] = stack16(q_ref[:, k : k + step])
    for r in range(RANK):
        wide_q[r] = jnp.broadcast_to(q_ref[r : r + 1, split:], (8, width - split))

    def pool_bias():
        heads = groups_ref.shape[1]
        local_heads = bias_ref.shape[0]
        first = lax.axis_index("tensor") * local_heads
        head = lax.broadcasted_iota(jnp.int32, (NG, heads), 1)
        member = groups_ref[...] == lax.broadcasted_iota(jnp.int32, (NG, heads), 0)
        count = jnp.sum(jnp.where(member, 1.0, 0.0), axis=1, keepdims=True)
        mine = jnp.where(member & (head >= first) & (head < first + local_heads), 1.0, 0.0).astype(BF16)
        rows_of_all = jnp.concatenate([bias_ref[...]] * (heads // local_heads), axis=0)
        pooled = sum(jnp.dot(mine, piece.astype(BF16), preferred_element_type=F32) for piece in reversed(split3(rows_of_all)))
        bias_out[...] = pooled / (count * replicas)

    lane = lax.broadcasted_iota(jnp.int32, (strip, LANES), 1)

    def add_block(b):
        for start in range(b * block, (b + 1) * block, strip):
            at = slice(start, start + strip)
            sums = [jnp.zeros((strip // 8, 8, LANES), F32)] * RANK
            for k in range(split, width, LANES):
                merged = grads_ref[at, k : k + LANES].astype(F32) + errors_ref[at, k : k + LANES].astype(F32)
                merged = merged.reshape(strip // 8, 8, LANES)
                q_at = slice(k - split, k - split + LANES)
                sums = [sums[r] + merged * wide_q[r, :, q_at][None] for r in range(RANK)]
            columns = jnp.zeros((strip, LANES), F32)
            for r in range(RANK):
                column = jnp.sum(sums[r].reshape(strip, LANES), axis=1, keepdims=True)
                columns = jnp.where(lane == r, column, columns)
            sums_ref[at, :] = columns

    def product(b):
        at = slice(b * block, (b + 1) * block)
        terms = [
            lax.dot_general(q16_ref[...], held[at, 0:split], (((1,), (1,)), ((), ())), preferred_element_type=F32)
            for held in (grads_ref, errors_ref)
        ]
        return fold16(terms[0] + terms[1])

    terms = []
    for b in range(blocks):
        for copy in fetches(b):
            copy.wait()
        if b == blocks - 1:
            fetch_groups.wait()
            fetch_bias.wait()
            pool_bias()
        terms.append(product(b))
        add_block(b)
    left = jnp.concatenate(terms, axis=1) + sums_ref[...].T[0:RANK]
    left_ref[...] = jnp.broadcast_to(left[None], left_ref.shape)


def right_kernel(chunk, shards, replicas, bias_ref, left_terms, grads_ref, errors_ref, left_out, send_ref):
    n = send_ref.shape[0]
    width = grads_ref.shape[1]
    left = butterfly_sum([left_terms[r] for r in range(left_terms.shape[0])]) / replicas
    left_out[...] = left
    left16 = stack16(left)

    sub = lax.broadcasted_iota(jnp.int32, (RANK, LANES), 0)
    lane = lax.broadcasted_iota(jnp.int32, (RANK, LANES), 1)
    spread = jnp.zeros((RANK, LANES), F32)
    for i in range(RANK):
        column = jnp.sum(left * left[i : i + 1], axis=1, keepdims=True)
        spread += jnp.where(lane == RANK * i + sub, column, 0.0)
    gram_row = jnp.sum(spread, axis=0, keepdims=True)

    pieces = chunk // LANES
    bias_rows = NG // shards
    used = RANK * pieces
    per_step = max(1, 1536 // chunk)
    for start in range(0, n, per_step):
        cols = slice(start * chunk, min((start + per_step) * chunk, width))
        if cols.start < width:
            y16 = jnp.dot(left16, grads_ref[:, cols], preferred_element_type=F32)
            y16 += jnp.dot(left16, errors_ref[:, cols], preferred_element_type=F32)
            y = fold16(y16)
        for j in range(start, min(start + per_step, n)):
            for k in range(pieces):
                at = (j - start) * chunk + k * LANES
                if j * chunk < width:
                    send_ref[j, RANK * k : RANK * (k + 1), :] = y[:, at : at + LANES]
                else:
                    send_ref[j, RANK * k : RANK * (k + 1), :] = jnp.zeros((RANK, LANES), F32)
            group = (j % shards) * bias_rows
            send_ref[j, used : used + bias_rows, :] = bias_ref[group : group + bias_rows, :]
            send_ref[j, used + bias_rows : used + bias_rows + 1, :] = gram_row


def solve_kernel(chunk, bias_rows, replicas, left_ref, got_ref, p_ref, q_ref, bias_ref):
    n = got_ref.shape[0]
    copies = q_ref.shape[0]
    pieces = chunk // LANES
    used = RANK * pieces
    total = butterfly_sum([got_ref[j] for j in range(n)])
    bias_ref[...] = total[used : used + bias_rows]
    gram_row = total[used + bias_rows : used + bias_rows + 1] / replicas
    lane = lax.broadcasted_iota(jnp.int32, (1, LANES), 1)

    def entry(i, j):
        return jnp.sum(jnp.where(lane == RANK * i + j, gram_row, 0.0), axis=1, keepdims=True)

    chol = {}
    for j in range(RANK):
        for i in range(j, RANK):
            value = entry(i, j)
            for k in range(j):
                value = value - chol[i, k] * chol[j, k]
            chol[i, j] = jnp.sqrt(value) if i == j else value / chol[j, j]

    def forward(rows):
        solved = []
        for i in range(RANK):
            row = rows[i]
            for k in range(i):
                row = row - chol[i, k] * solved[k]
            solved.append(row / chol[i, i])
        return solved

    left = left_ref[...]
    for i, row in enumerate(forward([left[i : i + 1] for i in range(RANK)])):
        p_ref[i : i + 1, :] = row
    for k in range(pieces):
        part = total[RANK * k : RANK * (k + 1)] / replicas
        for i, row in enumerate(forward([part[i : i + 1] for i in range(RANK)])):
            q_ref[:, i : i + 1, k * LANES : (k + 1) * LANES] = jnp.broadcast_to(row[None], (copies, 1, LANES))


def errors_kernel(chunk, block, p_ref, bias_ref, q_chunks, grads_ref, errors_ref, out_hbm, p_hbm, q_hbm, bias_hbm, q_ref, q32_ref, out_ref, small_sems, sems):
    rows, width = grads_ref.shape
    copies = [
        pltpu.make_async_copy(p_ref, p_hbm, small_sems.at[0]),
        pltpu.make_async_copy(bias_ref, bias_hbm, small_sems.at[1]),
    ]
    for copy in copies:
        copy.start()
    p_high, p_mid, p_low = split3(p_ref[...])
    zero = jnp.zeros_like(p_high)
    p32 = jnp.concatenate([p_high, p_high, p_mid, p_high, p_low, p_mid, zero, zero], axis=0).T.astype(BF16)
    for j in range(width // chunk):
        q = q_chunks[j]
        cols = slice(j * chunk, (j + 1) * chunk)
        q_ref[:, cols] = q
        q_high, q_mid, q_low = split3(q)
        none = jnp.zeros_like(q)
        q32_ref[:, cols] = jnp.concatenate([q_high, q_mid, q_high, q_low, q_high, q_mid, none, none], axis=0).astype(BF16)
    copies.append(pltpu.make_async_copy(q_ref, q_hbm, small_sems.at[2]))
    copies[-1].start()
    step = width // 8
    for b in range(rows // block):
        at = slice(b * block, (b + 1) * block)
        for s in range(width // step):
            cols = slice(s * step, (s + 1) * step)
            approx = jnp.dot(p32[at], q32_ref[:, cols], preferred_element_type=F32)
            merged = grads_ref[at, cols].astype(F32) + errors_ref[at, cols].astype(F32)
            out_ref[at, cols] = (merged - approx).astype(BF16)
        to = pl.ds(b * block, block)
        copy = pltpu.make_async_copy(out_ref.at[to], out_hbm.at[to], sems.at[b])
        copy.start(priority=b % 2)
        copies.append(copy)
    for copy in copies:
        copy.wait()


def per_device(grads, errors, q_init, bias_grads, head_group):
    replicas, shards = lax.axis_size("dp"), lax.axis_size("tensor")
    n = replicas * shards
    _, rows, width = grads.shape
    chunk = LANES * math.ceil(width / (LANES * n))
    bias_rows = NG // shards
    send_rows = 8 * math.ceil((RANK * chunk // LANES + bias_rows + 1) / 8)
    vmem = pl.BlockSpec(memory_space=pltpu.VMEM)
    smem = pl.BlockSpec(memory_space=pltpu.SMEM)
    anywhere = pl.BlockSpec(memory_space=pl.ANY)
    block = 32

    held = pltpu.VMEM((rows, width), BF16)
    left, bias, held_grads, held_errors = pl.pallas_call(
        functools.partial(left_kernel, rows // 4, float(replicas)),
        out_shape=(pltpu.VMEM((replicas, RANK, rows), F32), pltpu.VMEM((NG, HD), F32), held, held),
        in_specs=[anywhere] * 5,
        out_specs=[vmem] * 4,
        scratch_shapes=[
            pltpu.VMEM((1, head_group.shape[0]), jnp.int32),
            pltpu.VMEM((RANK, width), F32),
            pltpu.VMEM((16, width * 9 // 16), BF16),
            pltpu.VMEM((RANK, 8, width - width * 9 // 16), F32),
            pltpu.VMEM((bias_grads.shape[1] // HD, HD), F32),
            pltpu.VMEM((rows, LANES), F32),
            pltpu.SemaphoreType.DMA((3,)),
            pltpu.SemaphoreType.DMA((2, 4)),
        ],
        compiler_params=pltpu.CompilerParams(vmem_limit_bytes=8 * MIB),
        name="left_term",
    )(*(pltpu.with_memory_space_constraint(x, pltpu.HBM) for x in (head_group.reshape(1, -1), q_init, bias_grads.reshape(-1, HD), grads[0], errors[0])))
    left_terms = lax.all_to_all(left, "dp", 0, 0, tiled=True)

    left, send = pl.pallas_call(
        functools.partial(right_kernel, chunk, shards, float(replicas)),
        out_shape=(jax.ShapeDtypeStruct((RANK, rows), F32), jax.ShapeDtypeStruct((n, send_rows, LANES), F32)),
        in_specs=[vmem] * 4,
        out_specs=[vmem] * 2,
        compiler_params=pltpu.CompilerParams(vmem_limit_bytes=16 * MIB),
        name="right_term",
    )(bias, left_terms, held_grads, held_errors)
    got = lax.all_to_all(send, ("dp", "tensor"), 0, 0, tiled=True)

    p, q_send, bias = pl.pallas_call(
        functools.partial(solve_kernel, chunk, bias_rows, float(replicas)),
        out_shape=(
            jax.ShapeDtypeStruct((RANK, rows), F32),
            jax.ShapeDtypeStruct((n, RANK, chunk), F32),
            jax.ShapeDtypeStruct((bias_rows, HD), F32),
        ),
        in_specs=[vmem] * 2,
        out_specs=[vmem] * 3,
        compiler_params=pltpu.CompilerParams(vmem_limit_bytes=16 * MIB),
        name="solve",
    )(left, got)
    q_chunks = lax.all_to_all(q_send, ("dp", "tensor"), 0, 0, tiled=True)

    new_errors, p_factor, q_factor, bias_update = pl.pallas_call(
        functools.partial(errors_kernel, chunk, block),
        out_shape=(
            jax.ShapeDtypeStruct((rows, width), BF16),
            jax.ShapeDtypeStruct((RANK, rows), F32),
            jax.ShapeDtypeStruct((RANK, width), F32),
            jax.ShapeDtypeStruct((bias_rows, HD), F32),
        ),
        in_specs=[vmem] * 5,
        out_specs=[anywhere] * 4,
        scratch_shapes=[
            pltpu.VMEM((RANK, width), F32),
            pltpu.VMEM((32, width), BF16),
            pltpu.VMEM((rows, width), BF16),
            pltpu.SemaphoreType.DMA((3,)),
            pltpu.SemaphoreType.DMA((rows // block,)),
        ],
        compiler_params=pltpu.CompilerParams(vmem_limit_bytes=24 * MIB),
        name="new_errors",
    )(p, bias, q_chunks, held_grads, held_errors)
    return (new_errors[None], p_factor, q_factor, bias_update.reshape(-1))


def solution(mesh):
    placed = (P("dp", "tensor", None), P("dp", "tensor", None), P(), P("dp", "tensor"), P())
    return jax.shard_map(
        per_device,
        mesh=mesh,
        in_specs=placed,
        out_specs=(P("dp", "tensor", None), P(None, "tensor"), P(), P("tensor")),
        check_vma=False,
    )
```

time: 208 us -> 51.7 us (0.25)
  waiting for transfers between devices: 82.9 us -> 0 us
  matrix products: 39.5 us -> 0 us
  blocking collectives: 64.4 us -> 37.4 us
  Pallas kernels: 0 us -> 13.5 us
  between operations: 14.1 us -> 0.65 us
  other arithmetic: 3.19 us -> 0 us
    psum x1 -> x0, waiting for transfers between devices: 82.9 us -> none  [per_device(): q_total, bias_total = lax.psum((q_part, bias_part), ('dp', 'tensor'))]
    psum x3 -> x0, blocking collectives: 64.4 us -> none  [the longest x1 36.2 us: per_device(): q_total, bias_total = lax.psum((q_part, bias_part), ('dp', 'tensor'))]
    dot_general x5 -> x0, matrix products: 39.3 us -> none  [the longest x1 15.2 us: per_device(): lax.dot_general(p_factor, q_factor, (((0,), (0,)), ((), ())), precision=h...]
    all_to_all x0 -> x3, blocking collectives: none -> 37.4 us  [the longest x1 13.9 us: per_device(): got = lax.all_to_all(send, ('dp', 'tensor'), 0, 0, tiled=True)]
    pallas_call x0 -> x4, Pallas kernels: none -> 13.5 us  [the longest x1 8.04 us: per_device(): pl.pallas_call(functools.partial(left_kernel, rows // 4, float(replicas))...]
  transfers between devices with their start and end apart: 1 -> 0, of which waited for: 1 -> 0; matrix products, arithmetic and copies ran while one was open for 0% -> 0% of each run, Pallas kernels for 0% -> 0%
where the time goes in v1:
time: 51.7 us; the launch traced here: 51.5 us
  blocking collectives  37.4 us (72%)
  Pallas kernels  13.5 us (26%)
  between operations  0.65 us (1%)
    all_to_all x1, blocking collectives, per_device(): got = lax.all_to_all(send, ('dp', 'tensor'), 0, 0, tiled=True)  13.9 us
    all_to_all x1, blocking collectives, per_device(): q_chunks = lax.all_to_all(q_send, ('dp', 'tensor'), 0, 0, tiled=True)  11.8 us
    all_to_all x1, blocking collectives, per_device(): left_terms = lax.all_to_all(left, 'dp', 0, 0, tiled=True)  11.7 us
    pallas_call x1, Pallas kernels, per_device(): pl.pallas_call(functools.partial(left_kernel, rows // 4, float(replicas))...  8.04 us
    pallas_call x1, Pallas kernels, per_device(): pl.pallas_call(functools.partial(errors_kernel, chunk, block), out_shape=...  3.48 us
    pallas_call x1, Pallas kernels, per_device(): pl.pallas_call(functools.partial(right_kernel, chunk, shards, float(repli...  1.75 us

profile of v1, /device:TPU:1, one launch (start us, length us, event | category | flops | bytes accessed | tf_op | source)
XLA Modules:
  0.0 51.5 jit_solution(6012351562654849671)
XLA Ops:
  0.6 8.0 %left_term.1 = (f32[8,4,256]{2,1,0:T(4,128)S(1)}, f32[8,128]{1,0:T(8,128)S(1)}, bf16[256,12288]{1,0:T(8,128)(2,1)S(1)}, bf16[256,12288]{1,0:T(8,128)(2,1)S(1)}) custom-call(s32[1,96]{1,0:T(1,128)} %bitcast.9, f32[4,12288]{1,0:T(4,128)} %q_hbm.1, f32[24,128]{1,0:T(8,128)} %bitcast.8, bf16[256,12288]{1,0:T(8,128)(2,1)} %bitcast.6, bf16[256,12288]{1,0:T(8,128)(2,1)} %bitcast.7), custom_call_target="tpu_custom_call" | custom-call | tf_op jit(solution)/shard_map/left_term/pallas_call | solution.py:247
  8.7 11.7 %all_to_all.15.left_terms = f32[8,4,256]{2,1,0:T(4,128)S(1)} all-to-all(f32[8,4,256]{2,1,0:T(4,128)S(1)} %get-tuple-element.18), channel_id=1, replica_groups=mesh['dp'=8,'tensor'=4] {'dp'}, dimensions={0} | all-to-all | bytes 65536 | tf_op jit(solution)/shard_map/all_to_all | solution.py:265
  20.4 1.7 %right_term.1 = (f32[4,256]{1,0:T(4,128)S(1)}, f32[32,16,128]{2,1,0:T(8,128)S(1)}) custom-call(f32[8,128]{1,0:T(8,128)S(1)} %get-tuple-element.17.bias_ref, f32[8,4,256]{2,1,0:T(4,128)S(1)} %all_to_all.15.left_terms, bf16[256,12288]{1,0:T(8,128)(2,1)S(1)} %get-tuple-element.19.grads_ref, bf16[256,12288]{1,0:T(8,128)(2,1)S(1)} %get-tuple-element.20.errors_ref), custom_call_target="tpu_custom_call" | custom-call | tf_op jit(solution)/shard_map/right_term/pallas_call | solution.py:267
  22.1 13.9 %all_to_all.16.got_ref = f32[32,16,128]{2,1,0:T(8,128)S(1)} all-to-all(f32[32,16,128]{2,1,0:T(8,128)S(1)} %get-tuple-element.22), channel_id=1, replica_groups=mesh['dp'=8,'tensor'=4] {'dp','tensor'}, dimensions={0} | all-to-all | bytes 524288 | tf_op jit(solution)/shard_map/all_to_all | solution.py:275
  36.0 0.2 solve.1
  36.3 11.8 %all_to_all.17.q_chunks = f32[32,4,384]{2,1,0:T(4,128)S(1)} all-to-all(f32[32,4,384]{2,1,0:T(4,128)S(1)} %get-tuple-element.25), channel_id=1, replica_groups=mesh['dp'=8,'tensor'=4] {'dp','tensor'}, dimensions={0} | all-to-all | bytes 393216 | tf_op jit(solution)/shard_map/all_to_all | solution.py:289
  48.0 3.5 %new_errors.1 = (bf16[256,12288]{1,0:T(8,128)(2,1)}, f32[4,256]{1,0:T(4,128)}, f32[4,12288]{1,0:T(4,128)}, f32[2,128]{1,0:T(2,128)}) custom-call(f32[4,256]{1,0:T(4,128)S(1)} %get-tuple-element.23.p_ref, f32[2,128]{1,0:T(2,128)S(1)} %get-tuple-element.24.bias_ref, f32[32,4,384]{2,1,0:T(4,128)S(1)} %all_to_all.17.q_chunks, ...), custom_call_target="tpu_custom_call" | custom-call | tf_op jit(solution)/shard_map/new_errors/pallas_call | solution.py:291

commit v2 on v1

--- a/solution.py
+++ b/solution.py
@@ -39,10 +39,11 @@
     return parts[0]
 
 
-def left_kernel(block, replicas, groups_hbm, q_hbm, bias_hbm, grads_hbm, errors_hbm, left_ref, bias_out, grads_ref, errors_ref, groups_ref, q_ref, q16_ref, wide_q, bias_ref, sums_ref, small_sems, sems):
+def left_kernel(replicas, groups_hbm, q_hbm, bias_hbm, grads_hbm, errors_hbm, left_ref, bias_out, grads_ref, errors_ref, groups_ref, q_ref, q16_ref, wide_q, bias_ref, sums_ref, small_sems, sems):
     rows, width = grads_hbm.shape
     strip = 32
-    blocks = rows // block
+    edges = [0, rows * 3 // 8 // strip * strip, rows * 3 // 4 // strip * strip, rows]
+    blocks = [slice(i, j) for i, j in zip(edges, edges[1:])]
     split = width * 9 // 16
     fetch_q = pltpu.make_async_copy(q_hbm, q_ref, small_sems.at[0])
     fetch_groups = pltpu.make_async_copy(groups_hbm, groups_ref, small_sems.at[1])
@@ -50,13 +51,13 @@
     fetch_q.start(priority=1)
 
     def fetches(b):
-        at = pl.ds(b * block, block)
+        at = pl.ds(blocks[b].start, blocks[b].stop - blocks[b].start)
         return (
             pltpu.make_async_copy(grads_hbm.at[at], grads_ref.at[at], sems.at[0, b]),
             pltpu.make_async_copy(errors_hbm.at[at], errors_ref.at[at], sems.at[1, b]),
         )
 
-    for b in range(blocks):
+    for b in range(len(blocks)):
         for queue, copy in enumerate(fetches(b)):
             copy.start(priority=queue)
     fetch_groups.start(priority=0)
@@ -83,7 +84,7 @@
     lane = lax.broadcasted_iota(jnp.int32, (strip, LANES), 1)
 
     def add_block(b):
-        for start in range(b * block, (b + 1) * block, strip):
+        for start in range(blocks[b].start, blocks[b].stop, strip):
             at = slice(start, start + strip)
             sums = [jnp.zeros((strip // 8, 8, LANES), F32)] * RANK
             for k in range(split, width, LANES):
@@ -98,7 +99,7 @@
             sums_ref[at, :] = columns
 
     def product(b):
-        at = slice(b * block, (b + 1) * block)
+        at = blocks[b]
         terms = [
             lax.dot_general(q16_ref[...], held[at, 0:split], (((1,), (1,)), ((), ())), preferred_element_type=F32)
             for held in (grads_ref, errors_ref)
@@ -106,10 +107,10 @@
         return fold16(terms[0] + terms[1])
 
     terms = []
-    for b in range(blocks):
+    for b in range(len(blocks)):
         for copy in fetches(b):
             copy.wait()
-        if b == blocks - 1:
+        if b == len(blocks) - 1:
             fetch_groups.wait()
             fetch_bias.wait()
             pool_bias()
@@ -245,7 +246,7 @@
 
     held = pltpu.VMEM((rows, width), BF16)
     left, bias, held_grads, held_errors = pl.pallas_call(
-        functools.partial(left_kernel, rows // 4, float(replicas)),
+        functools.partial(left_kernel, float(replicas)),
         out_shape=(pltpu.VMEM((replicas, RANK, rows), F32), pltpu.VMEM((NG, HD), F32), held, held),
         in_specs=[anywhere] * 5,
         out_specs=[vmem] * 4,
@@ -257,7 +258,7 @@
             pltpu.VMEM((bias_grads.shape[1] // HD, HD), F32),
             pltpu.VMEM((rows, LANES), F32),
             pltpu.SemaphoreType.DMA((3,)),
-            pltpu.SemaphoreType.DMA((2, 4)),
+            pltpu.SemaphoreType.DMA((2, 3)),
         ],
         compiler_params=pltpu.CompilerParams(vmem_limit_bytes=8 * MIB),
         name="left_term",

time: 51.7 us -> 51.5 us (level)
  no operation moved by 1% of the time
where the time goes in v2:
time: 51.5 us; the launch traced here: 51.3 us
  blocking collectives  37.4 us (73%)
  Pallas kernels  13.3 us (26%)
  between operations  0.65 us (1%)
    all_to_all x1, blocking collectives, per_device(): got = lax.all_to_all(send, ('dp', 'tensor'), 0, 0, tiled=True)  13.9 us
    all_to_all x1, blocking collectives, per_device(): q_chunks = lax.all_to_all(q_send, ('dp', 'tensor'), 0, 0, tiled=True)  11.8 us
    all_to_all x1, blocking collectives, per_device(): left_terms = lax.all_to_all(left, 'dp', 0, 0, tiled=True)  11.7 us
    pallas_call x1, Pallas kernels, per_device(): pl.pallas_call(functools.partial(left_kernel, float(replicas)), out_shape...  7.83 us
    pallas_call x1, Pallas kernels, per_device(): pl.pallas_call(functools.partial(errors_kernel, chunk, block), out_shape=...  3.48 us
    pallas_call x1, Pallas kernels, per_device(): pl.pallas_call(functools.partial(right_kernel, chunk, shards, float(repli...  1.75 us

profile of v2, /device:TPU:1, one launch (start us, length us, event | category | flops | bytes accessed | tf_op | source)
XLA Modules:
  0.0 51.3 jit_solution(17543698040617130528)
XLA Ops:
  0.6 7.8 %left_term.1 = (f32[8,4,256]{2,1,0:T(4,128)S(1)}, f32[8,128]{1,0:T(8,128)S(1)}, bf16[256,12288]{1,0:T(8,128)(2,1)S(1)}, bf16[256,12288]{1,0:T(8,128)(2,1)S(1)}) custom-call(s32[1,96]{1,0:T(1,128)} %bitcast.9, f32[4,12288]{1,0:T(4,128)} %q_hbm.1, f32[24,128]{1,0:T(8,128)} %bitcast.8, bf16[256,12288]{1,0:T(8,128)(2,1)} %bitcast.6, bf16[256,12288]{1,0:T(8,128)(2,1)} %bitcast.7), custom_call_target="tpu_custom_call" | custom-call | tf_op jit(solution)/shard_map/left_term/pallas_call | solution.py:248
  8.5 11.7 %all_to_all.15.left_terms = f32[8,4,256]{2,1,0:T(4,128)S(1)} all-to-all(f32[8,4,256]{2,1,0:T(4,128)S(1)} %get-tuple-element.18), channel_id=1, replica_groups=mesh['dp'=8,'tensor'=4] {'dp'}, dimensions={0} | all-to-all | bytes 65536 | tf_op jit(solution)/shard_map/all_to_all | solution.py:266
  20.2 1.7 %right_term.1 = (f32[4,256]{1,0:T(4,128)S(1)}, f32[32,16,128]{2,1,0:T(8,128)S(1)}) custom-call(f32[8,128]{1,0:T(8,128)S(1)} %get-tuple-element.17.bias_ref, f32[8,4,256]{2,1,0:T(4,128)S(1)} %all_to_all.15.left_terms, bf16[256,12288]{1,0:T(8,128)(2,1)S(1)} %get-tuple-element.19.grads_ref, bf16[256,12288]{1,0:T(8,128)(2,1)S(1)} %get-tuple-element.20.errors_ref), custom_call_target="tpu_custom_call" | custom-call | tf_op jit(solution)/shard_map/right_term/pallas_call | solution.py:268
  21.9 13.9 %all_to_all.16.got_ref = f32[32,16,128]{2,1,0:T(8,128)S(1)} all-to-all(f32[32,16,128]{2,1,0:T(8,128)S(1)} %get-tuple-element.22), channel_id=1, replica_groups=mesh['dp'=8,'tensor'=4] {'dp','tensor'}, dimensions={0} | all-to-all | bytes 524288 | tf_op jit(solution)/shard_map/all_to_all | solution.py:276
  35.8 0.2 solve.1
  36.0 11.8 %all_to_all.17.q_chunks = f32[32,4,384]{2,1,0:T(4,128)S(1)} all-to-all(f32[32,4,384]{2,1,0:T(4,128)S(1)} %get-tuple-element.25), channel_id=1, replica_groups=mesh['dp'=8,'tensor'=4] {'dp','tensor'}, dimensions={0} | all-to-all | bytes 393216 | tf_op jit(solution)/shard_map/all_to_all | solution.py:290
  47.8 3.5 %new_errors.1 = (bf16[256,12288]{1,0:T(8,128)(2,1)}, f32[4,256]{1,0:T(4,128)}, f32[4,12288]{1,0:T(4,128)}, f32[2,128]{1,0:T(2,128)}) custom-call(f32[4,256]{1,0:T(4,128)S(1)} %get-tuple-element.23.p_ref, f32[2,128]{1,0:T(2,128)S(1)} %get-tuple-element.24.bias_ref, f32[32,4,384]{2,1,0:T(4,128)S(1)} %all_to_all.17.q_chunks, ...), custom_call_target="tpu_custom_call" | custom-call | tf_op jit(solution)/shard_map/new_errors/pallas_call | solution.py:292
